TPU v7x, 32 devices: a whole 2x2x4 slice. The times are simulated.
32 devices in a mesh: replica: 8 (over y, x, core), fsdp: 4 (over z).
Axes of the slice: x: 2, y: 2, z: 4, core: 2. Of those that a mesh axis runs over, the one named last changes fastest.
Arguments:
- weights: bfloat16 [8, 4096, 512], P('replica', 'fsdp'), may hold values from -6 to 6
- pseudo_grad: bfloat16 [8, 4096, 512], P('replica', 'fsdp'), may hold values from -6 to 6
- momentum: bfloat16 [8, 4096, 512], P('replica', 'fsdp'), may hold values from -6 to 6
- partner: int32 [8], replicated, may hold values from 0 to 7, as said below
- activations: bfloat16 [8192, 4096], P('replica', 'fsdp'), may hold values from -6 to 6
- key_cotangent: bfloat16 [8192, 512], P(('replica', 'fsdp')), may hold values from -0.1875 to 0.1875
Outputs:
- new_weights: bfloat16 [8, 4096, 512], P('replica', 'fsdp')
- new_momentum: bfloat16 [8, 4096, 512], P('replica', 'fsdp')
- weight_grad: bfloat16 [8, 4096, 512], P('replica', 'fsdp')
Inputs may be any that keep to these rules, and one draw needn't show every extreme that they name: partner is a matching: partner[partner[r]] = r and partner[r] != r for every replica r.
All inputs are finite; a program needn't handle non-finite values.
Results may differ from a plain program's by a relative error of at most 0.001.
Values may be sent and summed in bfloat16 or wider, within the bound.
A program may use at most 64 MiB of HBM per device.

v0:
```python
import functools

import jax
import jax.numpy as jnp
from jax import lax
from jax.experimental import pallas as pl
from jax.experimental.pallas import tpu as pltpu
from jax.sharding import PartitionSpec as P

CHUNKS = 4
ROW_TILE = 16
MIB = 1 << 20

decay_old = 0.5
grad_rate = 0.7
pull_rate = 0.9


def remote(src, dst, send_sem, recv_sem, **where):
    return pltpu.make_async_remote_copy(
        src_ref=src,
        dst_ref=dst,
        send_sem=send_sem,
        recv_sem=recv_sem,
        device_id=where,
        device_id_type=pl.DeviceIdType.MESH,
    )


def kernel(n, p, chunks, partner, weights, grad, momentum, acts, cotan,
           new_weights, new_momentum, weight_grad, *scratch):
    holds = scratch[:chunks]
    (routed, arrived, w_v, g_v, m_v, a_v, k_v, nw_v, nm_v, wg_v,
     spread_send, spread_recv, collect_send, collect_recv,
     k_send, k_recv, local_sem, self_sem, out_sem) = scratch[chunks:]
    me = lax.axis_index("replica")
    mz = lax.axis_index("fsdp")
    tok = cotan.shape[0]
    pieces = (weights, grad)

    barrier = pltpu.get_barrier_semaphore()

    @pl.loop(1, n)
    def _(d):
        pl.semaphore_signal(barrier, inc=1, device_id={"replica": lax.rem(me + d, n)},
                            device_id_type=pl.DeviceIdType.MESH)

    @pl.loop(1, p)
    def _(d):
        pl.semaphore_signal(barrier, inc=1, device_id={"fsdp": lax.rem(mz + d, p)},
                            device_id_type=pl.DeviceIdType.MESH)

    self_copies = []
    for c in range(chunks):
        for i in range(2):
            cp = pltpu.make_async_copy(pieces[i].at[me, c], holds[c].at[i, me], self_sem.at[c, i])
            cp.start()
            self_copies.append(cp)
    k_rows = pl.ds(pl.multiple_of(mz * tok, tok), tok)
    local_copies = [
        pltpu.make_async_copy(cotan, k_v.at[k_rows], local_sem.at[0]),
        pltpu.make_async_copy(weights, w_v, local_sem.at[1]),
        pltpu.make_async_copy(grad, g_v, local_sem.at[2]),
        pltpu.make_async_copy(momentum, m_v, local_sem.at[3]),
        pltpu.make_async_copy(acts, a_v, local_sem.at[4]),
    ]
    for cp in local_copies:
        cp.start()

    pl.semaphore_wait(barrier, n - 1 + p - 1)

    def spread(c, i, to):
        return remote(pieces[i].at[to, c], holds[c].at[i, me],
                      spread_send.at[c, i, to], spread_recv.at[c, i, me], replica=to)

    def spread_in(c, i, frm):
        return remote(pieces[i].at[frm, c], holds[c].at[i, frm],
                      spread_send.at[c, i, frm], spread_recv.at[c, i, frm], replica=frm)

    def collect(c, to):
        return remote(routed.at[c, to], arrived.at[c, me],
                      collect_send.at[c, to], collect_recv.at[c, me], replica=to)

    def collect_in(c, frm):
        return remote(routed.at[c, frm], arrived.at[c, frm],
                      collect_send.at[c, frm], collect_recv.at[c, frm], replica=frm)

    def share(to):
        return remote(cotan, k_v.at[k_rows], k_send.at[to], k_recv.at[mz], fsdp=to)

    def share_in(frm):
        rows = pl.ds(pl.multiple_of(frm * tok, tok), tok)
        return remote(cotan, k_v.at[rows], k_send.at[frm], k_recv.at[frm], fsdp=frm)

    for c in range(chunks):
        @pl.loop(1, n)
        def _(d, c=c):
            to = lax.rem(me + d, n)
            spread(c, 0, to).start()
            spread(c, 1, to).start()

        if c == 0:
            @pl.loop(1, p)
            def _(d):
                share(lax.rem(mz + d, p)).start()

    for c in range(chunks):
        self_copies[2 * c].wait()
        self_copies[2 * c + 1].wait()

        @pl.loop(1, n)
        def _(d, c=c):
            frm = lax.rem(me + n - d, n)
            spread_in(c, 0, frm).wait_recv()
            spread_in(c, 1, frm).wait_recv()

        @pl.loop(1, n)
        def _(d, c=c):
            to = lax.rem(me + d, n)
            source = partner[to]
            routed[c, to, 0] = holds[c][0, source]
            routed[c, to, 1] = holds[c][1, source]
            collect(c, to).start()

        source = partner[me]
        arrived[c, me, 0] = holds[c][0, source]
        arrived[c, me, 1] = holds[c][1, source]

    for cp in local_copies:
        cp.wait()

    @pl.loop(1, p)
    def _(d):
        share_in(lax.rem(mz + p - d, p)).wait_recv()

    feats = a_v.shape[1]
    step = 256 if feats % 256 == 0 else feats

    @pl.loop(0, feats // step)
    def _(t):
        cols = pl.ds(pl.multiple_of(t * step, step), step)
        wg_v[cols, :] = lax.dot_general(
            a_v[:, cols], k_v[...], (((0,), (0,)), ((), ())),
            preferred_element_type=jnp.float32).astype(wg_v.dtype)

    wg_out = pltpu.make_async_copy(wg_v, weight_grad, out_sem.at[2, 0])
    wg_out.start()

    out_copies = [wg_out]
    for c in range(chunks):
        @pl.loop(0, n)
        def _(d, c=c):
            frm = lax.rem(me + n - d, n)

            @pl.when(d > 0)
            def _():
                collect_in(c, frm).wait_recv()

            w = w_v[frm, c].astype(jnp.float32)
            g = g_v[frm, c].astype(jnp.float32)
            mean_w = (w + arrived[c, frm, 0].astype(jnp.float32)) * 0.5
            mean_g = (g + arrived[c, frm, 1].astype(jnp.float32)) * 0.5
            mom = (decay_old * m_v[frm, c].astype(jnp.float32)
                   - grad_rate * mean_g - pull_rate * (w - mean_w))
            nw_v[frm, c] = (w + decay_old * mom - grad_rate * mean_g).astype(nw_v.dtype)
            nm_v[frm, c] = mom.astype(nm_v.dtype)

        for i, (src, dst) in enumerate(((nw_v, new_weights), (nm_v, new_momentum))):
            cp = pltpu.make_async_copy(src.at[:, c], dst.at[:, c], out_sem.at[i, c])
            cp.start()
            out_copies.append(cp)

    for c in range(chunks):
        @pl.loop(1, n)
        def _(d, c=c):
            to = lax.rem(me + d, n)
            spread(c, 0, to).wait_send()
            spread(c, 1, to).wait_send()
            collect(c, to).wait_send()

    @pl.loop(1, p)
    def _(d):
        share(lax.rem(mz + d, p)).wait_send()

    for cp in out_copies:
        cp.wait()


def on_device(weights, pseudo_grad, momentum, partner, activations, key_cotangent):
    n, p = lax.axis_size("replica"), lax.axis_size("fsdp")
    rows, cols = weights.shape[1:]
    chunks = CHUNKS if rows >= n * CHUNKS * ROW_TILE else 1
    piece = -(-rows // (n * chunks * ROW_TILE)) * ROW_TILE
    padded = n * chunks * piece
    view = (n, chunks, piece, cols)

    def cut(x):
        x = x[0]
        if padded != rows:
            x = jnp.pad(x, ((0, padded - rows), (0, 0)))
        return x.reshape(view)

    def join(x):
        return x.reshape(padded, cols)[:rows][None]

    bf16 = jnp.bfloat16
    tokens, feats = activations.shape
    out_view = jax.ShapeDtypeStruct(view, bf16)
    any_space = pl.BlockSpec(memory_space=pl.ANY)
    dma = pltpu.SemaphoreType.DMA
    new_weights, new_momentum, weight_grad = pl.pallas_call(
        functools.partial(kernel, n, p, chunks),
        out_shape=(out_view, out_view, jax.ShapeDtypeStruct((feats, cols), bf16)),
        in_specs=[pl.BlockSpec(memory_space=pltpu.SMEM)] + [any_space] * 5,
        out_specs=(any_space,) * 3,
        scratch_shapes=[pltpu.VMEM((2, n, piece, cols), bf16) for _ in range(chunks)] + [
            pltpu.VMEM((chunks, n, 2, piece, cols), bf16),
            pltpu.VMEM((chunks, n, 2, piece, cols), bf16),
            pltpu.VMEM(view, bf16),
            pltpu.VMEM(view, bf16),
            pltpu.VMEM(view, bf16),
            pltpu.VMEM((tokens, feats), bf16),
            pltpu.VMEM((tokens, cols), bf16),
            pltpu.VMEM(view, bf16),
            pltpu.VMEM(view, bf16),
            pltpu.VMEM((feats, cols), bf16),
            dma((chunks, 2, n)),
            dma((chunks, 2, n)),
            dma((chunks, n)),
            dma((chunks, n)),
            dma((p,)),
            dma((p,)),
            dma((5,)),
            dma((chunks, 2)),
            dma((3, chunks)),
        ],
        compiler_params=pltpu.CompilerParams(
            collective_id=0, has_side_effects=True, vmem_limit_bytes=62 * MIB),
        cost_estimate=pl.CostEstimate(
            flops=2 * tokens * feats * cols, bytes_accessed=20 * rows * cols, transcendentals=0),
    )(partner, cut(weights), cut(pseudo_grad), cut(momentum), activations, key_cotangent)
    return join(new_weights), join(new_momentum), weight_grad[None]


def solution(mesh):
    return jax.shard_map(
        on_device,
        mesh=mesh,
        in_specs=(
            P("replica", "fsdp", None),
            P("replica", "fsdp", None),
            P("replica", "fsdp", None),
            P(),
            P("replica", "fsdp"),
            P(("replica", "fsdp"), None),
        ),
        out_specs=(
            P("replica", "fsdp", None),
            P("replica", "fsdp", None),
            P("replica", "fsdp", None),
        ),
        check_vma=False,
    )
```

profile of v0, /device:TPU:1, one launch (start us, length us, event | category | flops | bytes accessed | tf_op | source)
XLA Modules:
  0.0 60.3 jit_solution(6877638704902412647)
XLA Ops:
  0.6 55.3 %shard_map.85 = (bf16[8,4,32,512]{3,2,1,0:T(8,128)(2,1)}, bf16[8,4,32,512]{3,2,1,0:T(8,128)(2,1)}, bf16[1024,512]{1,0:T(8,128)(2,1)}) custom-call(s32[8]{0:T(128)} %partner.1, bf16[8,4,32,512]{3,2,1,0:T(8,128)(2,1)} %bitcast.9, bf16[8,4,32,512]{3,2,1,0:T(8,128)(2,1)} %bitcast.10, bf16[8,4,32,512]{3,2,1,0:T(8,128)(2,1)} %bitcast.11, bf16[1024,1024]{1,0:T(8,128)(2,1)} %acts.1, ...), custom_call_target="tpu_custom_call" | custom-call | flops 1073741824 | bytes 10485760 | tf_op jit(solution)/shard_map/pallas_call | solution.py:211
  55.9 0.0 copy-start.1
  56.0 0.0 copy-start
  56.0 2.4 %copy.12 = bf16[1,1024,512]{2,1,0:T(8,128)(2,1)} copy(bf16[1,1024,512]{2,1,0:T(8,128)(2,1)} %bitcast.8) | data formatting | bytes 2097152
  58.4 0.0 copy-done.1
  58.4 1.0 %copy.13 = bf16[1,1024,512]{2,1,0:T(8,128)(2,1)} copy(bf16[1,1024,512]{2,1,0:T(8,128)(2,1)S(1)} %bitcast.7) | data formatting | bytes 2097152
  59.3 0.0 copy-done
  59.3 1.0 %copy.14 = bf16[1,1024,512]{2,1,0:T(8,128)(2,1)} copy(bf16[1,1024,512]{2,1,0:T(8,128)(2,1)S(1)} %bitcast.6) | data formatting | bytes 2097152
Async XLA Ops:
  55.9 2.4 %copy-start.1 = (bf16[8,4,32,512]{3,2,1,0:T(8,128)(2,1)S(1)}, bf16[8,4,32,512]{3,2,1,0:T(8,128)(2,1)}, u32[]{:S(2)}) copy-start(bf16[8,4,32,512]{3,2,1,0:T(8,128)(2,1)} %get-tuple-element.7) | copy-start | bytes 3145732
  56.0 3.4 %copy-start = (bf16[1024,512]{1,0:T(8,128)(2,1)S(1)}, bf16[1024,512]{1,0:T(8,128)(2,1)}, u32[]{:S(2)}) copy-start(bf16[1024,512]{1,0:T(8,128)(2,1)} %get-tuple-element.8) | copy-start | bytes 3145732
where the time goes:
time: 60.5 us; the launch traced here: 60.3 us
  Pallas kernels  55.3 us (91%)
  local copies, waits for them, and re-layouts  4.36 us (7%)
  between operations  0.66 us (1%)
    pallas_call x1, Pallas kernels, on_device(): pl.pallas_call(functools.partial(kernel, n, p, chunks), out_shape=(out_vi...  55.3 us
    unnamed x7, local copies, waits for them, and re-layouts  4.36 us

commit v1 on v0

--- a/solution.py
+++ b/solution.py
@@ -8,6 +8,7 @@
 from jax.sharding import PartitionSpec as P
 
 CHUNKS = 4
+LANE_CHUNKS = 16
 ROW_TILE = 16
 MIB = 1 << 20
 
@@ -25,6 +26,28 @@
         device_id=where,
         device_id_type=pl.DeviceIdType.MESH,
     )
+
+
+def update(w, g, m, partner_w, partner_g):
+    f32 = jnp.float32
+    w, g = w.astype(f32), g.astype(f32)
+    mean_w = (w + partner_w.astype(f32)) * 0.5
+    mean_g = (g + partner_g.astype(f32)) * 0.5
+    mom = decay_old * m.astype(f32) - grad_rate * mean_g - pull_rate * (w - mean_w)
+    new_w = w + decay_old * mom - grad_rate * mean_g
+    return new_w.astype(jnp.bfloat16), mom.astype(jnp.bfloat16)
+
+
+def multiply(a_v, k_v, wg_v):
+    feats = a_v.shape[1]
+    step = 256 if feats % 256 == 0 else feats
+
+    @pl.loop(0, feats // step)
+    def _(t):
+        cols = pl.ds(pl.multiple_of(t * step, step), step)
+        wg_v[cols, :] = lax.dot_general(
+            a_v[:, cols], k_v[...], (((0,), (0,)), ((), ())),
+            preferred_element_type=jnp.float32).astype(wg_v.dtype)
 
 
 def kernel(n, p, chunks, partner, weights, grad, momentum, acts, cotan,
@@ -133,16 +156,7 @@
     def _(d):
         share_in(lax.rem(mz + p - d, p)).wait_recv()
 
-    feats = a_v.shape[1]
-    step = 256 if feats % 256 == 0 else feats
-
-    @pl.loop(0, feats // step)
-    def _(t):
-        cols = pl.ds(pl.multiple_of(t * step, step), step)
-        wg_v[cols, :] = lax.dot_general(
-            a_v[:, cols], k_v[...], (((0,), (0,)), ((), ())),
-            preferred_element_type=jnp.float32).astype(wg_v.dtype)
-
+    multiply(a_v, k_v, wg_v)
     wg_out = pltpu.make_async_copy(wg_v, weight_grad, out_sem.at[2, 0])
     wg_out.start()
 
@@ -156,14 +170,8 @@
             def _():
                 collect_in(c, frm).wait_recv()
 
-            w = w_v[frm, c].astype(jnp.float32)
-            g = g_v[frm, c].astype(jnp.float32)
-            mean_w = (w + arrived[c, frm, 0].astype(jnp.float32)) * 0.5
-            mean_g = (g + arrived[c, frm, 1].astype(jnp.float32)) * 0.5
-            mom = (decay_old * m_v[frm, c].astype(jnp.float32)
-                   - grad_rate * mean_g - pull_rate * (w - mean_w))
-            nw_v[frm, c] = (w + decay_old * mom - grad_rate * mean_g).astype(nw_v.dtype)
-            nm_v[frm, c] = mom.astype(nm_v.dtype)
+            nw_v[frm, c], nm_v[frm, c] = update(
+                w_v[frm, c], g_v[frm, c], m_v[frm, c], arrived[c, frm, 0], arrived[c, frm, 1])
 
         for i, (src, dst) in enumerate(((nw_v, new_weights), (nm_v, new_momentum))):
             cp = pltpu.make_async_copy(src.at[:, c], dst.at[:, c], out_sem.at[i, c])
@@ -186,60 +194,295 @@
         cp.wait()
 
 
-def on_device(weights, pseudo_grad, momentum, partner, activations, key_cotangent):
-    n, p = lax.axis_size("replica"), lax.axis_size("fsdp")
-    rows, cols = weights.shape[1:]
+def lane_kernel(p, chunks, groups, partner, weights, grad, momentum, acts, cotan,
+                new_weights, new_momentum, weight_grad,
+                own, rx, ry, tx, ty, handed, taken, w_v, g_v, m_v, a_v, k_v, nw_v, nm_v, wg_v,
+                x_send, x_recv, y_send, y_recv, pair_send, pair_recv, hand_send, hand_recv,
+                k_send, k_recv, local_sem, own_sem, out_sem):
+    me = lax.axis_index("replica")
+    mz = lax.axis_index("fsdp")
+    core, chip = lax.rem(me, 2), lax.div(me, 2)
+    x_chip = chip + 1 - 2 * lax.rem(chip, 2)
+    y_chip = chip + 2 - 4 * lax.div(chip, 2)
+    x_dev, y_dev, twin = 2 * x_chip + core, 2 * y_chip + core, 2 * chip + 1 - core
+    tok = cotan.shape[0]
+    pieces = (weights, grad)
+
+    barrier = pltpu.get_barrier_semaphore()
+    for peer in (x_dev, y_dev, twin):
+        pl.semaphore_signal(barrier, inc=1, device_id={"replica": peer},
+                            device_id_type=pl.DeviceIdType.MESH)
+
+    @pl.loop(1, p)
+    def _(d):
+        pl.semaphore_signal(barrier, inc=1, device_id={"fsdp": lax.rem(mz + d, p)},
+                            device_id_type=pl.DeviceIdType.MESH)
+
+    def own_copy(j, i):
+        at = pl.ds(groups[j][0], groups[j][1])
+        return pltpu.make_async_copy(
+            pieces[i].at[core, at], own.at[core, i, at], own_sem.at[j, i])
+
+    for j in range(len(groups)):
+        own_copy(j, 0).start()
+        own_copy(j, 1).start()
+    k_rows = pl.ds(pl.multiple_of(mz * tok, tok), tok)
+    local_copies = [
+        pltpu.make_async_copy(cotan, k_v.at[k_rows], local_sem.at[0]),
+        pltpu.make_async_copy(weights, w_v, local_sem.at[1]),
+        pltpu.make_async_copy(grad, g_v, local_sem.at[2]),
+        pltpu.make_async_copy(momentum, m_v, local_sem.at[3]),
+        pltpu.make_async_copy(acts, a_v, local_sem.at[4]),
+    ]
+
+    low, high = jnp.minimum(x_chip, y_chip), jnp.maximum(x_chip, y_chip)
+    low_closed = partner[2 * low] == 2 * low + 1
+    high_closed = partner[2 * high] == 2 * high + 1
+
+    def route(i):
+        j = partner[i]
+        there = lax.div(j, 2)
+        first = lax.rem(jnp.where(there < chip, j, i), 2)
+        by_high = jnp.logical_and(high_closed,
+                                  jnp.logical_or(jnp.logical_not(low_closed), first == 1))
+        by = jnp.where(by_high, high, low)
+        corner = jnp.where(by == x_chip, 3, 4)
+        return jnp.where(there == chip, 0,
+                         jnp.where(there == x_chip, 1, jnp.where(there == y_chip, 2, corner)))
+
+    def starts_x(code):
+        return jnp.logical_or(code == 1, code == 3)
+
+    def starts_y(code):
+        return jnp.logical_or(code == 2, code == 4)
+
+    code0, code1 = route(2 * chip), route(2 * chip + 1)
+    code_me, code_twin = route(me), route(twin)
+
+    pl.semaphore_wait(barrier, 3 + p - 1)
+
+    def pair(j, i):
+        at = pl.ds(groups[j][0], groups[j][1])
+        return remote(pieces[i].at[1 - core, at], own.at[core, i, at],
+                      pair_send.at[j, i], pair_recv.at[j, i], replica=twin)
+
+    def pair_in(j, i):
+        at = pl.ds(groups[j][0], groups[j][1])
+        return remote(pieces[i].at[1 - core, at], own.at[1 - core, i, at],
+                      pair_send.at[j, i], pair_recv.at[j, i], replica=twin)
+
+    def link_x(t):
+        return remote(tx.at[t], rx.at[t], x_send.at[t], x_recv.at[t], replica=x_dev)
+
+    def link_y(t):
+        return remote(ty.at[t], ry.at[t], y_send.at[t], y_recv.at[t], replica=y_dev)
+
+    def hand(c):
+        return remote(handed.at[c], taken.at[c], hand_send.at[c], hand_recv.at[c], replica=twin)
+
+    def share(to):
+        return remote(cotan, k_v.at[k_rows], k_send.at[to], k_recv.at[mz], fsdp=to)
+
+    def share_in(frm):
+        rows = pl.ds(pl.multiple_of(frm * tok, tok), tok)
+        return remote(cotan, k_v.at[rows], k_send.at[frm], k_recv.at[frm], fsdp=frm)
+
+    for j in range(len(groups)):
+        pair(j, 0).start()
+        pair(j, 1).start()
+        if j == 0:
+            @pl.loop(1, p)
+            def _(d):
+                share(lax.rem(mz + d, p)).start()
+    for cp in local_copies:
+        cp.start()
+
+    def pick(code, near, c):
+        far = lax.select(code == 3, rx[c + 2], ry[c + 2])
+        far = lax.select(code == 2, ry[c], far)
+        far = lax.select(code == 1, rx[c], far)
+        return lax.select(code == 0, near, far)
+
+    out_copies = []
+
+    def settle(half, c, got):
+        nw_v[half, c], nm_v[half, c] = update(
+            w_v[half, c], g_v[half, c], m_v[half, c], got[0], got[1])
+
+    def finish(c):
+        hand(c).wait_recv()
+        settle(1 - core, c, taken[c])
+        if c % 4 == 3:
+            at = pl.ds(c - 3, 4)
+            for i, (src, dst) in enumerate(((nw_v, new_weights), (nm_v, new_momentum))):
+                cp = pltpu.make_async_copy(src.at[:, at], dst.at[:, at], out_sem.at[i, c // 4])
+                cp.start()
+                out_copies.append(cp)
+
+    def deliver(c):
+        handed[c] = pick(code_twin, own[core, :, c], c)
+        hand(c).start()
+        settle(core, c, pick(code_me, own[1 - core, :, c], c))
+        if c >= 2:
+            finish(c - 2)
+
+    for t in range(chunks + 2):
+        for j, (at, _) in enumerate(groups):
+            if at == t:
+                for i in range(2):
+                    own_copy(j, i).wait()
+                    pair_in(j, i).wait_recv()
+        if t < chunks:
+            block0, block1 = own[0, :, t], own[1, :, t]
+        if t >= 2:
+            link_x(t - 2).wait_recv()
+            link_y(t - 2).wait_recv()
+            out_x, out_y = ry[t - 2], rx[t - 2]
+        else:
+            out_x, out_y = block1, block1
+        if t < chunks:
+            out_x = lax.select(starts_x(code0), block0, lax.select(starts_x(code1), block1, out_x))
+            out_y = lax.select(starts_y(code0), block0, lax.select(starts_y(code1), block1, out_y))
+        tx[t] = out_x
+        link_x(t).start()
+        ty[t] = out_y
+        link_y(t).start()
+        if t == 4:
+            for cp in local_copies:
+                cp.wait()
+        if t >= 4:
+            deliver(t - 4)
+
+    @pl.loop(1, p)
+    def _(d):
+        share_in(lax.rem(mz + p - d, p)).wait_recv()
+
+    multiply(a_v, k_v, wg_v)
+    wg_out = pltpu.make_async_copy(wg_v, weight_grad, out_sem.at[2, 0])
+    wg_out.start()
+    out_copies.append(wg_out)
+
+    for t in (chunks, chunks + 1):
+        link_x(t).wait_recv()
+        link_y(t).wait_recv()
+        deliver(t - 2)
+    finish(chunks - 2)
+    finish(chunks - 1)
+
+    for t in range(chunks + 2):
+        link_x(t).wait_send()
+        link_y(t).wait_send()
+    for c in range(chunks):
+        hand(c).wait_send()
+    for j in range(len(groups)):
+        pair(j, 0).wait_send()
+        pair(j, 1).wait_send()
+
+    @pl.loop(1, p)
+    def _(d):
+        share(lax.rem(mz + d, p)).wait_send()
+
+    for cp in out_copies:
+        cp.wait()
+
+
+def call(body, identity, view, operands, scratch):
+    partner, weights, grad, momentum, acts, cotan = operands
+    bf16 = jnp.bfloat16
+    (tokens, feats), cols = acts.shape, cotan.shape[1]
+    out_view = jax.ShapeDtypeStruct(view, bf16)
+    any_space = pl.BlockSpec(memory_space=pl.ANY)
+    return pl.pallas_call(
+        body,
+        out_shape=(out_view, out_view, jax.ShapeDtypeStruct((feats, cols), bf16)),
+        in_specs=[pl.BlockSpec(memory_space=pltpu.SMEM)] + [any_space] * 5,
+        out_specs=(any_space,) * 3,
+        scratch_shapes=scratch,
+        compiler_params=pltpu.CompilerParams(
+            collective_id=identity, has_side_effects=True, vmem_limit_bytes=62 * MIB),
+        cost_estimate=pl.CostEstimate(
+            flops=2 * tokens * feats * cols, bytes_accessed=20 * weights.size // weights.shape[0],
+            transcendentals=0),
+    )(partner, weights.reshape(view), grad.reshape(view), momentum.reshape(view), acts, cotan)
+
+
+def spread_form(n, p, weights, pseudo_grad, momentum, partner, activations, key_cotangent):
+    rows, cols = weights.shape
     chunks = CHUNKS if rows >= n * CHUNKS * ROW_TILE else 1
     piece = -(-rows // (n * chunks * ROW_TILE)) * ROW_TILE
     padded = n * chunks * piece
     view = (n, chunks, piece, cols)
 
     def cut(x):
-        x = x[0]
-        if padded != rows:
-            x = jnp.pad(x, ((0, padded - rows), (0, 0)))
-        return x.reshape(view)
+        return jnp.pad(x, ((0, padded - rows), (0, 0))) if padded != rows else x
 
     def join(x):
-        return x.reshape(padded, cols)[:rows][None]
+        return x.reshape(padded, cols)[:rows]
 
     bf16 = jnp.bfloat16
     tokens, feats = activations.shape
-    out_view = jax.ShapeDtypeStruct(view, bf16)
-    any_space = pl.BlockSpec(memory_space=pl.ANY)
     dma = pltpu.SemaphoreType.DMA
-    new_weights, new_momentum, weight_grad = pl.pallas_call(
-        functools.partial(kernel, n, p, chunks),
-        out_shape=(out_view, out_view, jax.ShapeDtypeStruct((feats, cols), bf16)),
-        in_specs=[pl.BlockSpec(memory_space=pltpu.SMEM)] + [any_space] * 5,
-        out_specs=(any_space,) * 3,
-        scratch_shapes=[pltpu.VMEM((2, n, piece, cols), bf16) for _ in range(chunks)] + [
-            pltpu.VMEM((chunks, n, 2, piece, cols), bf16),
-            pltpu.VMEM((chunks, n, 2, piece, cols), bf16),
-            pltpu.VMEM(view, bf16),
-            pltpu.VMEM(view, bf16),
-            pltpu.VMEM(view, bf16),
-            pltpu.VMEM((tokens, feats), bf16),
-            pltpu.VMEM((tokens, cols), bf16),
-            pltpu.VMEM(view, bf16),
-            pltpu.VMEM(view, bf16),
-            pltpu.VMEM((feats, cols), bf16),
-            dma((chunks, 2, n)),
-            dma((chunks, 2, n)),
-            dma((chunks, n)),
-            dma((chunks, n)),
-            dma((p,)),
-            dma((p,)),
-            dma((5,)),
-            dma((chunks, 2)),
-            dma((3, chunks)),
-        ],
-        compiler_params=pltpu.CompilerParams(
-            collective_id=0, has_side_effects=True, vmem_limit_bytes=62 * MIB),
-        cost_estimate=pl.CostEstimate(
-            flops=2 * tokens * feats * cols, bytes_accessed=20 * rows * cols, transcendentals=0),
-    )(partner, cut(weights), cut(pseudo_grad), cut(momentum), activations, key_cotangent)
-    return join(new_weights), join(new_momentum), weight_grad[None]
+    vmem = pltpu.VMEM
+    scratch = [vmem((2, n, piece, cols), bf16) for _ in range(chunks)] + [
+        vmem((chunks, n, 2, piece, cols), bf16), vmem((chunks, n, 2, piece, cols), bf16),
+        vmem(view, bf16), vmem(view, bf16), vmem(view, bf16),
+        vmem((tokens, feats), bf16), vmem((tokens, cols), bf16),
+        vmem(view, bf16), vmem(view, bf16), vmem((feats, cols), bf16),
+        dma((chunks, 2, n)), dma((chunks, 2, n)), dma((chunks, n)), dma((chunks, n)),
+        dma((p,)), dma((p,)), dma((5,)), dma((chunks, 2)), dma((3, chunks)),
+    ]
+    new_weights, new_momentum, weight_grad = call(
+        functools.partial(kernel, n, p, chunks), 0, view,
+        (partner, cut(weights), cut(pseudo_grad), cut(momentum), activations, key_cotangent),
+        scratch)
+    return join(new_weights), join(new_momentum), weight_grad
+
+
+def lane_form(p, weights, pseudo_grad, momentum, partner, activations, key_cotangent):
+    rows, cols = weights.shape
+    chunks = LANE_CHUNKS
+    piece = rows // (2 * chunks)
+    view = (2, chunks, piece, cols)
+    groups = ((0, 1), (1, 1), (2, 2), (4, 4), (8, chunks - 8))
+    bf16 = jnp.bfloat16
+    tokens, feats = activations.shape
+    dma = pltpu.SemaphoreType.DMA
+    vmem = pltpu.VMEM
+    lane = vmem((chunks + 2, 2, piece, cols), bf16)
+    scratch = [
+        vmem((2, 2, chunks, piece, cols), bf16), lane, lane, lane, lane,
+        vmem((chunks, 2, piece, cols), bf16), vmem((chunks, 2, piece, cols), bf16),
+        vmem(view, bf16), vmem(view, bf16), vmem(view, bf16),
+        vmem((tokens, feats), bf16), vmem((tokens, cols), bf16),
+        vmem(view, bf16), vmem(view, bf16), vmem((feats, cols), bf16),
+        dma((chunks + 2,)), dma((chunks + 2,)), dma((chunks + 2,)), dma((chunks + 2,)),
+        dma((len(groups), 2)), dma((len(groups), 2)), dma((chunks,)), dma((chunks,)),
+        dma((p,)), dma((p,)), dma((5,)), dma((len(groups), 2)), dma((3, chunks // 4)),
+    ]
+    new_weights, new_momentum, weight_grad = call(
+        functools.partial(lane_kernel, p, chunks, groups), 1, view,
+        (partner, weights, pseudo_grad, momentum, activations, key_cotangent), scratch)
+    return new_weights.reshape(rows, cols), new_momentum.reshape(rows, cols), weight_grad
+
+
+def one_block_a_link(partner):
+    index = lax.iota(jnp.int32, 8)
+    over_x = (index // 2 + partner // 2) % 2
+    over_y = (index // 4 + partner // 4) % 2
+    crossings = jnp.sum(over_x + 16 * over_y)
+    return (crossings == 0) | (crossings == 4 * 17)
+
+
+def on_device(weights, pseudo_grad, momentum, partner, activations, key_cotangent):
+    n, p = lax.axis_size("replica"), lax.axis_size("fsdp")
+    operands = (weights[0], pseudo_grad[0], momentum[0], partner, activations, key_cotangent)
+    spread = functools.partial(spread_form, n, p)
+    if n == 8 and weights.shape[1] % (2 * LANE_CHUNKS * ROW_TILE) == 0:
+        outs = lax.cond(one_block_a_link(partner), functools.partial(lane_form, p), spread,
+                        *operands)
+    else:
+        outs = spread(*operands)
+    return tuple(out[None] for out in outs)
 
 
 def solution(mesh):

time: 60.5 us -> 50.8 us (0.84)
  Pallas kernels: 55.3 us -> 43.7 us
  other arithmetic: 0 us -> 1.31 us
  between operations: 0.66 us -> 1.96 us
  local copies, waits for them, and re-layouts: 4.36 us -> 3.53 us
    pallas_call x1, Pallas kernels: 55.3 us -> 43.7 us  [call(): pl.pallas_call(body, out_shape=(out_view, out_view, jax.ShapeDtypeStruct(...]
    reduce_sum x0 -> x1, other arithmetic: none -> 1.31 us  [one_block_a_link(): crossings = jnp.sum(over_x + 16 * over_y)]
    unnamed x7, local copies, waits for them, and re-layouts: 4.36 us -> 3.53 us
where the time goes in v1:
time: 50.8 us; the launch traced here: 50.6 us
  Pallas kernels  43.7 us (86%)
  local copies, waits for them, and re-layouts  3.53 us (7%)
  between operations  1.96 us (4%)
  other arithmetic  1.31 us (3%)
    pallas_call x1, Pallas kernels, call(): pl.pallas_call(body, out_shape=(out_view, out_view, jax.ShapeDtypeStruct(...  43.7 us
    unnamed x7, local copies, waits for them, and re-layouts  3.53 us
    reduce_sum x1, other arithmetic, one_block_a_link(): crossings = jnp.sum(over_x + 16 * over_y)  1.31 us

profile of v1, /device:TPU:1, one launch (start us, length us, event | category | flops | bytes accessed | tf_op | source)
XLA Modules:
  0.0 50.6 jit_solution(11703573876683899977)
XLA Ops:
  0.6 1.3 %fusion.6 = s32[]{:T(128)} fusion(s32[8]{0:T(128)} %param.11), kind=kLoop, calls=%fused_computation.26 | loop fusion | flops 527 | bytes 36 | tf_op jit(solution)/shard_map/reduce_sum | solution.py:472
  3.2 43.8 %conditional.1 = (bf16[1024,512]{1,0:T(8,128)(2,1)}, bf16[1,1024,512]{2,1,0:T(8,128)(2,1)S(1)}, bf16[1,1024,512]{2,1,0:T(8,128)(2,1)}) conditional(s32[]{:T(128)} %convert_element_type.3, (bf16[1,1024,512]{2,1,0:T(8,128)(2,1)}, bf16[1,1024,512]{2,1,0:T(8,128)(2,1)}, bf16[1,1024,512]{2,1,0:T(8,128)(2,1)}, s32[8]{0:T(128)}, ...), branch_computations={%region_1.2_spmd, %region_2.3_spmd} | conditional | flops 1073741824 | bytes 10264 | solution.py:481
  3.3 43.7 %branch_1_fun.1 = (bf16[2,16,32,512]{3,2,1,0:T(8,128)(2,1)S(1)}, bf16[2,16,32,512]{3,2,1,0:T(8,128)(2,1)}, bf16[1024,512]{1,0:T(8,128)(2,1)}) custom-call(s32[8]{0:T(128)} %get-tuple-element.35.partner, bf16[2,16,32,512]{3,2,1,0:T(8,128)(2,1)} %bitcast.12, bf16[2,16,32,512]{3,2,1,0:T(8,128)(2,1)} %bitcast.14, bf16[2,16,32,512]{3,2,1,0:T(8,128)(2,1)} %bitcast.16, ...), custom_call_target="tpu_custom_call" | custom-call | flops 1073741824 | bytes 10240 | tf_op jit(solution)/shard_map/cond/branch_1_fun/pallas_call | solution.py:395
  47.0 0.0 copy-start
  47.0 0.0 copy-start.1
  47.0 1.0 %copy.18 = bf16[1,1024,512]{2,1,0:T(8,128)(2,1)} copy(bf16[1,1024,512]{2,1,0:T(8,128)(2,1)S(1)} %get-tuple-element.62) | data formatting | bytes 2097152
  48.0 0.6 %copy-done = bf16[1,1024,512]{2,1,0:T(8,128)(2,1)S(1)} copy-done((bf16[1,1024,512]{2,1,0:T(8,128)(2,1)S(1)}, bf16[1,1024,512]{2,1,0:T(8,128)(2,1)}, u32[]{:S(2)}) %copy-start) | copy-done | bytes 1048600
  48.6 1.0 %copy.19 = bf16[1,1024,512]{2,1,0:T(8,128)(2,1)} copy(bf16[1,1024,512]{2,1,0:T(8,128)(2,1)S(1)} %copy-done) | data formatting | bytes 2097152
  49.6 0.0 copy-done.1
  49.6 1.0 %copy.20 = bf16[1,1024,512]{2,1,0:T(8,128)(2,1)} copy(bf16[1,1024,512]{2,1,0:T(8,128)(2,1)S(1)} %bitcast.21) | data formatting | bytes 2097152
Async XLA Ops:
  47.0 1.6 %copy-start = (bf16[1,1024,512]{2,1,0:T(8,128)(2,1)S(1)}, bf16[1,1024,512]{2,1,0:T(8,128)(2,1)}, u32[]{:S(2)}) copy-start(bf16[1,1024,512]{2,1,0:T(8,128)(2,1)} %get-tuple-element.63) | copy-start | bytes 3145732
  47.0 2.6 %copy-start.1 = (bf16[1024,512]{1,0:T(8,128)(2,1)S(1)}, bf16[1024,512]{1,0:T(8,128)(2,1)}, u32[]{:S(2)}) copy-start(bf16[1024,512]{1,0:T(8,128)(2,1)} %get-tuple-element.52) | copy-start | bytes 3145732
